TPU v7x, 128 devices: a whole 4x4x4 slice. The times are simulated.
128 devices in a mesh: wide: 8 (over y, core), col: 16 (over z, x).
Axes of the slice: x: 4, y: 4, z: 4, core: 2. Of those that a mesh axis runs over, the one named last changes fastest.
Arguments:
- rhs: float32 [98304, 256], P(('wide', 'col')), may hold values from -6 to 6
- basis: bfloat16 [98304, 256], P(('wide', 'col')), may hold values from -0.21875 to 0.21875
- self_block: bfloat16 [98304, 768], P(('wide', 'col'))
- near_block: bfloat16 [128, 8, 768, 768], P(('wide', 'col')), may hold values from -0.0546875 to 0.0546875
- near_ids: int32 [128, 8], P(('wide', 'col')), may hold values from -1 to 127, as said below
- couplings: bfloat16 [128, 40, 256, 256], P(('wide', 'col')), may hold values from -0.09375 to 0.09375
- far_ids: int32 [128, 40], P(('wide', 'col')), may hold values from -1 to 127, as said below
- intersection_start: int32 [128, 2], P(('wide', 'col')), may hold values from 0 to 512
- schwarz_inverse: bfloat16 [128, 1280, 1280], P(('wide', 'col'))
Outputs:
- solution: float32 [98304, 256], P(('wide', 'col'))
Inputs may be any that keep to these rules, and one draw needn't show every extreme that they name: `near_ids`: row c lists every cluster adjacent to cluster c on the grid (larger index distance 1; id = first index * 16 + second), ids first and -1 after them; rows of corner and edge clusters end in -1. `far_ids`: row c lists distinct clusters whose larger grid index distance from cluster c is 2 to 3, ids first and -1 after them; counts are ragged, and some rows list every such cluster. `intersection_start`: column 0 starts the rows taken by the domain of the cluster before along the second grid index, column 1 those taken by the one after.
All inputs are finite; a program needn't handle non-finite values.
Results may differ from a plain program's by a relative error of at most 0.0025.
The roundings to bfloat16 on the way count: a program that leaves them out, or rounds other values in their place, can miss the bound.
Values may be sent and summed in bfloat16 or wider, within the bound.
A program may use at most 128 MiB of HBM per device.

v0:
```python
import jax
import jax.numpy as jnp
from jax import lax
from jax.sharding import PartitionSpec as P

REACH = 3
ITERS = 2
HIGHEST_PREC = lax.Precision.HIGHEST
GROUP_SLOTS = 8


def passed_along(block, axis, distance):
    devices = range(lax.axis_size(axis))
    route = [(i - distance, i) for i in devices if i - distance in devices]
    return lax.ppermute(block, axis, route)


def with_halo(block, sides, width):
    for axis, dim in sides:
        count = lax.axis_size(axis)
        forward = [(i, i + 1) for i in range(count - 1)]
        backward = [(target, source) for source, target in forward]
        low = lax.ppermute(
            lax.slice_in_dim(block, block.shape[dim] - width, None, axis=dim), axis, forward
        )
        high = lax.ppermute(lax.slice_in_dim(block, 0, width, axis=dim), axis, backward)
        block = jnp.concatenate([low, block, high], axis=dim)
    return block


def local_gram(left, right):
    return lax.dot_general(
        left,
        right,
        (((0,), (0,)), ((), ())),
        precision=HIGHEST_PREC,
        preferred_element_type=jnp.float32,
    )


def lower_solve(factor, matrix):
    return lax.linalg.triangular_solve(
        factor, matrix, left_side=False, lower=True, transpose_a=True
    )


def far_window(coefficients):
    strip_row = jnp.stack(
        [
            coefficients if offset == 0 else passed_along(coefficients, "col", -offset)
            for offset in range(-REACH, REACH + 1)
        ]
    )
    window = jnp.stack(
        [
            strip_row if offset == 0 else passed_along(strip_row, "wide", -offset)
            for offset in range(-REACH, REACH + 1)
        ]
    )
    return window


def operate(vector_in, basis, self_block, near_block, near_ids, couplings, far_ids):
    rounded = vector_in.astype(jnp.bfloat16)
    cluster_rows, width = rounded.shape
    rank = basis.shape[1]
    wide_pos = lax.axis_index("wide")
    col_pos = lax.axis_index("col")
    col_count = lax.axis_size("col")
    result = jnp.dot(self_block, rounded, preferred_element_type=jnp.float32)
    beside_all = with_halo(rounded[None, None], (("wide", 0), ("col", 1)), 1)
    for slot_index in range(near_ids.shape[1]):
        neighbour = near_ids[0, slot_index]
        safe_id = jnp.maximum(neighbour, 0)
        wide_off = safe_id // col_count - wide_pos + 1
        col_off = safe_id % col_count - col_pos + 1
        other = lax.dynamic_slice(
            beside_all, (wide_off, col_off, 0, 0), (1, 1, cluster_rows, width)
        )[0, 0]
        product = jnp.dot(near_block[0, slot_index], other, preferred_element_type=jnp.float32)
        result = result + jnp.where(neighbour >= 0, product, jnp.zeros_like(product))
    coefficients = lax.dot_general(
        basis, rounded, (((0,), (0,)), ((), ())), preferred_element_type=jnp.float32
    ).astype(jnp.bfloat16)
    window = far_window(coefficients)
    span = 2 * REACH + 1
    flat_window = window.reshape(span * span, rank, width)
    far_list = far_ids[0]
    live_count = jnp.sum((far_list >= 0).astype(jnp.int32))
    group_count = (live_count + GROUP_SLOTS - 1) // GROUP_SLOTS

    def add_group(group_index, running):
        first_slot = group_index * GROUP_SLOTS
        targets = lax.dynamic_slice_in_dim(far_list, first_slot, GROUP_SLOTS, 0)
        safe_ids = jnp.maximum(targets, 0)
        flat_index = (safe_ids // col_count - wide_pos + REACH) * span + (
            safe_ids % col_count - col_pos + REACH
        )
        pieces_in = jnp.take(flat_window, flat_index, axis=0)
        coupling_group = lax.dynamic_slice_in_dim(couplings[0], first_slot, GROUP_SLOTS, 0)
        live_slots = (targets >= 0)[:, None, None]
        coupling_group = jnp.where(live_slots, coupling_group, jnp.zeros_like(coupling_group))
        return running + jnp.einsum(
            "lrs,lsk->rk", coupling_group, pieces_in, preferred_element_type=jnp.float32
        )

    far_sum = lax.fori_loop(0, group_count, add_group, jnp.zeros((rank, width), jnp.float32))
    return result + jnp.dot(basis, far_sum.astype(jnp.bfloat16), preferred_element_type=jnp.float32)


def add_rows(matrix, addend, start):
    current = lax.dynamic_slice_in_dim(matrix, start, addend.shape[0], 0)
    return lax.dynamic_update_slice_in_dim(matrix, current + addend, start, 0)


def precondition(vector_in, intersection_start, schwarz_inverse):
    rounded = vector_in.astype(jnp.bfloat16)
    cluster_rows = rounded.shape[0]
    margin = (schwarz_inverse.shape[1] - cluster_rows) // 2
    starts = intersection_start[0]
    prev_whole, prev_starts = passed_along((rounded, intersection_start), "col", 1)
    next_whole, next_starts = passed_along((rounded, intersection_start), "col", -1)
    prev_rows = lax.dynamic_slice_in_dim(prev_whole, prev_starts[0, 1], margin, 0)
    next_rows = lax.dynamic_slice_in_dim(next_whole, next_starts[0, 0], margin, 0)
    domain = jnp.concatenate([prev_rows, rounded, next_rows], axis=0)
    solved = jnp.dot(schwarz_inverse[0], domain, preferred_element_type=jnp.float32)
    result = solved[margin : margin + cluster_rows]
    from_next = passed_along(solved[:margin], "col", -1)
    from_prev = passed_along(solved[margin + cluster_rows :], "col", 1)
    result = add_rows(result, from_next, starts[1])
    result = add_rows(result, from_prev, starts[0])
    return result


def on_device(
    rhs,
    basis,
    self_block,
    near_block,
    near_ids,
    couplings,
    far_ids,
    intersection_start,
    schwarz_inverse,
):
    width = rhs.shape[1]
    first_sum = lax.psum(local_gram(rhs, rhs), ("wide", "col"))
    factor = jnp.linalg.cholesky(first_sum)
    beta_block = factor.T
    bases = [lower_solve(factor, rhs)]
    directions = []
    columns = []
    for iteration in range(ITERS):
        precond_out = precondition(bases[-1], intersection_start, schwarz_inverse)
        image = operate(precond_out, basis, self_block, near_block, near_ids, couplings, far_ids)
        stacked = jnp.concatenate(bases, axis=1)
        projected = lax.psum(local_gram(stacked, image), ("wide", "col"))
        image = image - jnp.dot(stacked, projected, precision=HIGHEST_PREC)
        gram_sum = lax.psum(local_gram(image, image), ("wide", "col"))
        factor = jnp.linalg.cholesky(gram_sum)
        columns.append((projected, factor.T))
        directions.append(precond_out)
        if iteration + 1 < ITERS:
            bases.append(lower_solve(factor, image))
    hessen = jnp.zeros(((ITERS + 1) * width, ITERS * width), jnp.float32)
    for column_index, (projected, sub_block) in enumerate(columns):
        upper_rows = (column_index + 1) * width
        hessen = hessen.at[:upper_rows, column_index * width : (column_index + 1) * width].set(
            projected
        )
        hessen = hessen.at[
            upper_rows : upper_rows + width, column_index * width : (column_index + 1) * width
        ].set(sub_block)
    normal_matrix = jnp.dot(hessen.T, hessen, precision=HIGHEST_PREC)
    target = jnp.dot(hessen[:width].T, beta_block, precision=HIGHEST_PREC)
    small_factor = jnp.linalg.cholesky(normal_matrix)
    middle = lax.linalg.triangular_solve(small_factor, target, left_side=True, lower=True)
    weights_y = lax.linalg.triangular_solve(
        small_factor, middle, left_side=True, lower=True, transpose_a=True
    )
    return jnp.dot(jnp.concatenate(directions, axis=1), weights_y, precision=HIGHEST_PREC)


def solution(mesh):
    in_specs = (
        P(("wide", "col"), None),
        P(("wide", "col"), None),
        P(("wide", "col"), None),
        P(("wide", "col"), None, None, None),
        P(("wide", "col"), None),
        P(("wide", "col"), None, None, None),
        P(("wide", "col"), None),
        P(("wide", "col"), None),
        P(("wide", "col"), None, None),
    )
    out_specs = P(("wide", "col"), None)
    return jax.shard_map(
        on_device, mesh=mesh, in_specs=in_specs, out_specs=out_specs, check_vma=False
    )
```

profile of v0, /device:TPU:1, one launch (start us, length us, event | category | flops | bytes accessed | tf_op | source)
XLA Modules:
  0.0 1556.4 jit_solution(12817224653365156530)
XLA Ops:
  10.3 146.7 %all-reduce.9.cloned.1.call-done = f32[256,256]{0,1:T(8,128)} async-done(((f32[256,256]{0,1:T(8,128)}), f32[256,256]{0,1:T(8,128)}) %all-reduce.9.cloned.1.call-update) | async-done | bytes 262160 | tf_op jit(solution)/shard_map/psum | solution.py:147
  159.7 11.7 cholesky.392
  172.1 10.4 custom-call.47
  186.2 13.2 cholesky.402
  203.7 7.4 while.36
  211.1 21.1 %custom-call.48 = f32[2,128,128]{1,2,0:T(8,128)} custom-call(f32[2,128,128]{2,1,0:T(8,128)} %get-tuple-element.295), custom_call_target="InvertDiagBlocksLowerTriangular" | custom-call | tf_op jit(solution)/shard_map/triangular_solve/custom-call.9 | solution.py:42
  242.7 4.0 collective-permute-start.1
  260.9 4.7 collective-permute-start.5
  281.5 8.3 collective-permute-start.10
  309.5 7.1 collective-permute-start.16
  339.1 19.0 %collective-permute-done.6 = bf16[1,1,768,256]{2,3,1,0:T(8,128)(2,1)} collective-permute-done((bf16[1,1,768,256]{2,3,1,0:T(8,128)(2,1)}, bf16[1,1,768,256]{2,3,1,0:T(8,128)(2,1)}, u32[]{:S(2)}, u32[]{:S(2)}) %collective-permute-start.6) | collective-permute-done | bytes 393248 | tf_op jit(solution)/shard_map/ppermute | solution.py:23
  367.2 5.0 collective-permute-start.8
  387.8 9.3 copy.13
  397.9 14.7 while.33
  398.0 4.4 gather_fusion
  405.4 4.4 gather_fusion
  428.6 185.3 %all-reduce.11.cloned.1.call-done = f32[256,256]{1,0:T(8,128)} async-done(((f32[256,256]{1,0:T(8,128)}), f32[256,256]{1,0:T(8,128)}) %all-reduce.11.cloned.1.call-update) | async-done | bytes 262160 | tf_op jit(solution)/shard_map/psum | solution.py:157
  618.9 138.9 %all-reduce.13.cloned.1.call-done = f32[256,256]{0,1:T(8,128)} async-done(((f32[256,256]{0,1:T(8,128)}), f32[256,256]{0,1:T(8,128)}) %all-reduce.13.cloned.1.call-update) | async-done | bytes 262160 | tf_op jit(solution)/shard_map/psum | solution.py:159
  762.0 13.2 cholesky.419
  778.2 11.3 custom-call.49
  792.9 13.2 cholesky.429
  812.6 7.5 while.37
  820.2 21.1 %custom-call.50 = f32[2,128,128]{1,2,0:T(8,128)} custom-call(f32[2,128,128]{2,1,0:T(8,128)} %get-tuple-element.296), custom_call_target="InvertDiagBlocksLowerTriangular" | custom-call | tf_op jit(solution)/shard_map/triangular_solve/custom-call.9 | solution.py:42
  850.6 6.0 collective-permute-done.22
  863.1 4.4 collective-permute-start.25
  875.1 9.7 collective-permute-start.30
  896.6 4.8 collective-permute-done.34
  904.8 8.3 collective-permute-start.36
  922.9 30.5 %collective-permute-done.26 = bf16[1,1,768,256]{2,3,1,0:T(8,128)(2,1)S(1)} collective-permute-done((bf16[1,1,768,256]{2,3,1,0:T(8,128)(2,1)S(1)}, bf16[1,1,768,256]{2,3,1,0:T(8,128)(2,1)S(1)}, u32[]{:S(2)}, u32[]{:S(2)}) %collective-permute-start.26) | collective-permute-done | bytes 393248 | tf_op jit(solution)/shard_map/ppermute | solution.py:23
  961.2 5.0 collective-permute-start.28
  983.0 9.3 copy.19
  993.1 12.1 while.34
  1023.1 184.5 %all-reduce.15.cloned.1.call-done = f32[512,256]{1,0:T(8,128)} async-done(((f32[512,256]{1,0:T(8,128)}), f32[512,256]{1,0:T(8,128)}) %all-reduce.15.cloned.1.call-update) | async-done | bytes 524304 | tf_op jit(solution)/shard_map/psum | solution.py:157
  1215.5 6.3 scatter.16
  1221.8 131.3 %all-reduce.17.cloned.1.call-done = f32[256,256]{0,1:T(8,128)} async-done(((f32[256,256]{0,1:T(8,128)}), f32[256,256]{0,1:T(8,128)}) %all-reduce.17.cloned.1.call-update) | async-done | bytes 262160 | tf_op jit(solution)/shard_map/psum | solution.py:159
  1355.2 11.7 cholesky.446
  1367.0 9.8 custom-call.51
  1377.2 11.7 cholesky.456
  1397.7 11.7 cholesky.167
  1409.5 9.8 custom-call.37
  1421.9 11.9 cholesky.190
  1435.1 9.8 custom-call.38
  1446.5 11.7 cholesky.294
  1459.0 9.8 custom-call.52
  1470.2 11.9 cholesky.307
  1485.6 10.6 while.35
  1496.2 40.2 %custom-call.39 = f32[4,128,128]{1,2,0:T(8,128)S(1)} custom-call(f32[4,128,128]{2,1,0:T(8,128)} %get-tuple-element.288), custom_call_target="InvertDiagBlocksLowerTriangular" | custom-call | tf_op jit(solution)/shard_map/triangular_solve | solution.py:178
  1544.8 4.9 fusion.36
  (391 shorter events, 310.4 us)
Async XLA Ops:
  6.5 150.4 %all-reduce.9.cloned.1.call-start = ((), (), s32[]{:S(2)}) async-start(), calls=%async_computation | async-start | bytes 524288 | tf_op jit(solution)/shard_map/psum | solution.py:147
  10.2 603.7 %all-reduce.11.cloned.1.call-start = ((), (), s32[]{:S(2)}) async-start(), calls=%async_computation.1 | async-start | bytes 524288 | tf_op jit(solution)/shard_map/psum | solution.py:157
  238.0 15.6 %collective-permute-start = (bf16[768,256]{0,1:T(8,128)(2,1)}, bf16[768,256]{0,1:T(8,128)(2,1)}, u32[]{:S(2)}, u32[]{:S(2)}) collective-permute-start(bf16[768,256]{0,1:T(8,128)(2,1)} %fusion.109), channel_id=1, source_target_pairs={{0,1},{1,2},{2,3},{3,4},{4,5},{5,6},{6,7},{7,8},{8,9},{9,10},{10,1... | collective-permute-start | bytes 1179656 | tf_op jit(solution)/shard_map/ppermute | solution.py:15
  241.4 13.3 collective-permute-start.2
  242.7 5.6 collective-permute-start.1
  246.7 6.2 collective-permute-start.3
  259.6 11.3 collective-permute-start.4
  260.9 14.9 collective-permute-start.5
  281.5 15.3 collective-permute-start.10
  289.8 9.0 collective-permute-start.11
  291.1 8.4 collective-permute-start.12
  294.2 6.9 collective-permute-start.13
  295.5 9.3 collective-permute-start.14
  296.8 12.0 collective-permute-start.15
  309.5 54.3 %collective-permute-start.16 = (bf16[7,256,256]{1,2,0:T(8,128)(2,1)}, bf16[7,256,256]{1,2,0:T(8,128)(2,1)}, u32[]{:S(2)}, u32[]{:S(2)}) collective-permute-start(bf16[7,256,256]{1,2,0:T(8,128)(2,1)} %bitcast_dynamic-update-slice_fusion.25), channel_id=1, source_target_pairs={{0,48},{16,64},{32,80},{48,96},{64,112},{1,49},{17,65},{33,81},{49... | collective-permute-start | bytes 2752520 | tf_op jit(solution)/shard_map/ppermute | solution.py:15
  316.5 50.7 %collective-permute-start.17 = (bf16[7,256,256]{1,2,0:T(8,128)(2,1)}, bf16[7,256,256]{1,2,0:T(8,128)(2,1)}, u32[]{:S(2)}, u32[]{:S(2)}) collective-permute-start(bf16[7,256,256]{1,2,0:T(8,128)(2,1)} %bitcast_dynamic-update-slice_fusion.25), channel_id=1, source_target_pairs={{0,32},{16,48},{32,64},{48,80},{64,96},{80,112},{1,33},{17,49},{33... | collective-permute-start | bytes 2752520 | tf_op jit(solution)/shard_map/ppermute | solution.py:15
  319.5 38.6 %collective-permute-start.6 = (bf16[1,1,768,256]{2,3,1,0:T(8,128)(2,1)}, bf16[1,1,768,256]{2,3,1,0:T(8,128)(2,1)}, u32[]{:S(2)}, u32[]{:S(2)}) collective-permute-start(bf16[1,1,768,256]{2,3,1,0:T(8,128)(2,1)} %convert_bitcast_fusion.1), channel_id=1, source_target_pairs={{0,16},{16,32},{32,48},{48,64},{64,80},{80,96},{96,112},{1,17},{17... | collective-permute-start | bytes 1179656 | tf_op jit(solution)/shard_map/ppermute | solution.py:23
  321.5 38.6 %collective-permute-start.7 = (bf16[1,1,768,256]{2,3,1,0:T(8,128)(2,1)}, bf16[1,1,768,256]{2,3,1,0:T(8,128)(2,1)}, u32[]{:S(2)}, u32[]{:S(2)}) collective-permute-start(bf16[1,1,768,256]{2,3,1,0:T(8,128)(2,1)} %convert_bitcast_fusion.1), channel_id=1, source_target_pairs={{16,0},{32,16},{48,32},{64,48},{80,64},{96,80},{112,96},{17,1},{33... | collective-permute-start | bytes 1179656 | tf_op jit(solution)/shard_map/ppermute | solution.py:26
  324.6 49.8 %collective-permute-start.18 = (bf16[7,256,256]{1,2,0:T(8,128)(2,1)}, bf16[7,256,256]{1,2,0:T(8,128)(2,1)}, u32[]{:S(2)}, u32[]{:S(2)}) collective-permute-start(bf16[7,256,256]{1,2,0:T(8,128)(2,1)} %bitcast_dynamic-update-slice_fusion.25), channel_id=1, source_target_pairs={{0,16},{16,32},{32,48},{48,64},{64,80},{80,96},{96,112},{1,17},{17... | collective-permute-start | bytes 2752520 | tf_op jit(solution)/shard_map/ppermute | solution.py:15
  358.2 23.7 %collective-permute-start.19 = (bf16[7,256,256]{1,2,0:T(8,128)(2,1)}, bf16[7,256,256]{1,2,0:T(8,128)(2,1)S(1)}, u32[]{:S(2)}, u32[]{:S(2)}) collective-permute-start(bf16[7,256,256]{1,2,0:T(8,128)(2,1)} %bitcast_dynamic-update-slice_fusion.25), channel_id=1, source_target_pairs={{16,0},{32,16},{48,32},{64,48},{80,64},{96,80},{112,96},{17,1},{33... | collective-permute-start | bytes 2752520 | tf_op jit(solution)/shard_map/ppermute | solution.py:15
  360.1 25.7 %collective-permute-start.20 = (bf16[7,256,256]{1,2,0:T(8,128)(2,1)}, bf16[7,256,256]{1,2,0:T(8,128)(2,1)S(1)}, u32[]{:S(2)}, u32[]{:S(2)}) collective-permute-start(bf16[7,256,256]{1,2,0:T(8,128)(2,1)} %bitcast_dynamic-update-slice_fusion.25), channel_id=1, source_target_pairs={{32,0},{48,16},{64,32},{80,48},{96,64},{112,80},{33,1},{49,17},{65... | collective-permute-start | bytes 2752520 | tf_op jit(solution)/shard_map/ppermute | solution.py:15
  363.8 23.0 %collective-permute-start.21 = (bf16[7,256,256]{1,2,0:T(8,128)(2,1)}, bf16[7,256,256]{1,2,0:T(8,128)(2,1)S(1)}, u32[]{:S(2)}, u32[]{:S(2)}) collective-permute-start(bf16[7,256,256]{1,2,0:T(8,128)(2,1)} %bitcast_dynamic-update-slice_fusion.25), channel_id=1, source_target_pairs={{48,0},{64,16},{80,32},{96,48},{112,64},{49,1},{65,17},{81,33},{97... | collective-permute-start | bytes 2752520 | tf_op jit(solution)/shard_map/ppermute | solution.py:15
  367.2 45.4 %collective-permute-start.8 = (bf16[3,1,768,256]{2,3,1,0:T(8,128)(2,1)}, bf16[3,1,768,256]{2,3,1,0:T(8,128)(2,1)}, u32[]{:S(2)}, u32[]{:S(2)}) collective-permute-start(bf16[3,1,768,256]{2,3,1,0:T(8,128)(2,1)} %pad_maximum_fusion.2), channel_id=1, source_target_pairs={{0,1},{1,2},{2,3},{3,4},{4,5},{5,6},{6,7},{7,8},{8,9},{9,10},{10,1... | collective-permute-start | bytes 3538952 | tf_op jit(solution)/shard_map/ppermute | solution.py:23
  374.4 38.2 %collective-permute-start.9 = (bf16[3,1,768,256]{2,3,1,0:T(8,128)(2,1)}, bf16[3,1,768,256]{2,3,1,0:T(8,128)(2,1)}, u32[]{:S(2)}, u32[]{:S(2)}) collective-permute-start(bf16[3,1,768,256]{2,3,1,0:T(8,128)(2,1)} %pad_maximum_fusion.2), channel_id=1, source_target_pairs={{1,0},{2,1},{3,2},{4,3},{5,4},{6,5},{7,6},{8,7},{9,8},{10,9},{11,1... | collective-permute-start | bytes 3538952 | tf_op jit(solution)/shard_map/ppermute | solution.py:26
  428.5 384.1 %copy-start.38 = (s32[2,2]{1,0:T(2,128)S(1)}, s32[2,2]{1,0:T(2,128)}, u32[]{:S(2)}) copy-start(s32[2,2]{1,0:T(2,128)} %copy-done.37) | copy-start | bytes 52
  428.5 329.3 %all-reduce.13.cloned.1.call-start = ((), (), s32[]{:S(2)}) async-start(), calls=%async_computation.2 | async-start | bytes 524288 | tf_op jit(solution)/shard_map/psum | solution.py:159
  618.6 589.0 %all-reduce.15.cloned.1.call-start = ((), (), s32[]{:S(2)}) async-start(), calls=%async_computation.3 | async-start | bytes 1048576 | tf_op jit(solution)/shard_map/psum | solution.py:157
  846.6 9.9 collective-permute-start.22
  849.3 11.2 collective-permute-start.23
  861.6 8.4 collective-permute-start.24
  863.1 9.3 collective-permute-start.25
  875.1 16.7 %collective-permute-start.30 = (bf16[256,256]{0,1:T(8,128)(2,1)S(1)}, bf16[256,256]{0,1:T(8,128)(2,1)S(1)}, u32[]{:S(2)}, u32[]{:S(2)}) collective-permute-start(bf16[256,256]{0,1:T(8,128)(2,1)S(1)} %bitcast.418), channel_id=1, source_target_pairs={{0,3},{1,4},{2,5},{3,6},{4,7},{5,8},{6,9},{7,10},{8,11},{9,12},{10... | collective-permute-start | bytes 393224 | tf_op jit(solution)/shard_map/ppermute | solution.py:15
  884.8 9.0 collective-permute-start.31
  886.4 8.1 collective-permute-start.32
  889.2 6.7 collective-permute-start.33
  890.5 10.8 collective-permute-start.34
  891.8 12.3 collective-permute-start.35
  904.8 52.9 %collective-permute-start.36 = (bf16[7,256,256]{1,2,0:T(8,128)(2,1)}, bf16[7,256,256]{1,2,0:T(8,128)(2,1)}, u32[]{:S(2)}, u32[]{:S(2)}) collective-permute-start(bf16[7,256,256]{1,2,0:T(8,128)(2,1)} %bitcast_dynamic-update-slice_fusion.19), channel_id=1, source_target_pairs={{0,48},{16,64},{32,80},{48,96},{64,112},{1,49},{17,65},{33,81},{49... | collective-permute-start | bytes 2752520 | tf_op jit(solution)/shard_map/ppermute | solution.py:15
  913.1 48.1 %collective-permute-start.37 = (bf16[7,256,256]{1,2,0:T(8,128)(2,1)}, bf16[7,256,256]{1,2,0:T(8,128)(2,1)}, u32[]{:S(2)}, u32[]{:S(2)}) collective-permute-start(bf16[7,256,256]{1,2,0:T(8,128)(2,1)} %bitcast_dynamic-update-slice_fusion.19), channel_id=1, source_target_pairs={{0,32},{16,48},{32,64},{48,80},{64,96},{80,112},{1,33},{17,49},{33... | collective-permute-start | bytes 2752520 | tf_op jit(solution)/shard_map/ppermute | solution.py:15
  915.3 38.0 %collective-permute-start.26 = (bf16[1,1,768,256]{2,3,1,0:T(8,128)(2,1)S(1)}, bf16[1,1,768,256]{2,3,1,0:T(8,128)(2,1)S(1)}, u32[]{:S(2)}, u32[]{:S(2)}) collective-permute-start(bf16[1,1,768,256]{2,3,1,0:T(8,128)(2,1)S(1)} %convert_bitcast_fusion), channel_id=1, source_target_pairs={{0,16},{16,32},{32,48},{48,64},{64,80},{80,96},{96,112},{1,17},{17... | collective-permute-start | bytes 1179656 | tf_op jit(solution)/shard_map/ppermute | solution.py:23
  917.3 38.0 %collective-permute-start.27 = (bf16[1,1,768,256]{2,3,1,0:T(8,128)(2,1)S(1)}, bf16[1,1,768,256]{2,3,1,0:T(8,128)(2,1)S(1)}, u32[]{:S(2)}, u32[]{:S(2)}) collective-permute-start(bf16[1,1,768,256]{2,3,1,0:T(8,128)(2,1)S(1)} %convert_bitcast_fusion), channel_id=1, source_target_pairs={{16,0},{32,16},{48,32},{64,48},{80,64},{96,80},{112,96},{17,1},{33... | collective-permute-start | bytes 1179656 | tf_op jit(solution)/shard_map/ppermute | solution.py:26
  919.7 48.7 %collective-permute-start.38 = (bf16[7,256,256]{1,2,0:T(8,128)(2,1)}, bf16[7,256,256]{1,2,0:T(8,128)(2,1)}, u32[]{:S(2)}, u32[]{:S(2)}) collective-permute-start(bf16[7,256,256]{1,2,0:T(8,128)(2,1)} %bitcast_dynamic-update-slice_fusion.19), channel_id=1, source_target_pairs={{0,16},{16,32},{32,48},{48,64},{64,80},{80,96},{96,112},{1,17},{17... | collective-permute-start | bytes 2752520 | tf_op jit(solution)/shard_map/ppermute | solution.py:15
  953.3 23.7 %collective-permute-start.39 = (bf16[7,256,256]{1,2,0:T(8,128)(2,1)}, bf16[7,256,256]{1,2,0:T(8,128)(2,1)S(1)}, u32[]{:S(2)}, u32[]{:S(2)}) collective-permute-start(bf16[7,256,256]{1,2,0:T(8,128)(2,1)} %bitcast_dynamic-update-slice_fusion.19), channel_id=1, source_target_pairs={{16,0},{32,16},{48,32},{64,48},{80,64},{96,80},{112,96},{17,1},{33... | collective-permute-start | bytes 2752520 | tf_op jit(solution)/shard_map/ppermute | solution.py:15
  955.3 25.7 %collective-permute-start.40 = (bf16[7,256,256]{1,2,0:T(8,128)(2,1)}, bf16[7,256,256]{1,2,0:T(8,128)(2,1)S(1)}, u32[]{:S(2)}, u32[]{:S(2)}) collective-permute-start(bf16[7,256,256]{1,2,0:T(8,128)(2,1)} %bitcast_dynamic-update-slice_fusion.19), channel_id=1, source_target_pairs={{32,0},{48,16},{64,32},{80,48},{96,64},{112,80},{33,1},{49,17},{65... | collective-permute-start | bytes 2752520 | tf_op jit(solution)/shard_map/ppermute | solution.py:15
  957.7 24.2 %collective-permute-start.41 = (bf16[7,256,256]{1,2,0:T(8,128)(2,1)}, bf16[7,256,256]{1,2,0:T(8,128)(2,1)S(1)}, u32[]{:S(2)}, u32[]{:S(2)}) collective-permute-start(bf16[7,256,256]{1,2,0:T(8,128)(2,1)} %bitcast_dynamic-update-slice_fusion.19), channel_id=1, source_target_pairs={{48,0},{64,16},{80,32},{96,48},{112,64},{49,1},{65,17},{81,33},{97... | collective-permute-start | bytes 2752520 | tf_op jit(solution)/shard_map/ppermute | solution.py:15
  961.2 44.0 %collective-permute-start.28 = (bf16[3,1,768,256]{2,3,1,0:T(8,128)(2,1)}, bf16[3,1,768,256]{2,3,1,0:T(8,128)(2,1)}, u32[]{:S(2)}, u32[]{:S(2)}) collective-permute-start(bf16[3,1,768,256]{2,3,1,0:T(8,128)(2,1)} %pad_maximum_fusion.3), channel_id=1, source_target_pairs={{0,1},{1,2},{2,3},{3,4},{4,5},{5,6},{6,7},{7,8},{8,9},{9,10},{10,1... | collective-permute-start | bytes 3538952 | tf_op jit(solution)/shard_map/ppermute | solution.py:23
  968.4 36.7 %collective-permute-start.29 = (bf16[3,1,768,256]{2,3,1,0:T(8,128)(2,1)}, bf16[3,1,768,256]{2,3,1,0:T(8,128)(2,1)}, u32[]{:S(2)}, u32[]{:S(2)}) collective-permute-start(bf16[3,1,768,256]{2,3,1,0:T(8,128)(2,1)} %pad_maximum_fusion.3), channel_id=1, source_target_pairs={{1,0},{2,1},{3,2},{4,3},{5,4},{6,5},{7,6},{8,7},{9,8},{10,9},{11,1... | collective-permute-start | bytes 3538952 | tf_op jit(solution)/shard_map/ppermute | solution.py:26
  1020.4 332.6 %all-reduce.17.cloned.1.call-start = ((), (), s32[]{:S(2)}) async-start(), calls=%async_computation.4 | async-start | bytes 524288 | tf_op jit(solution)/shard_map/psum | solution.py:159
  (44 other events, 971.7 us)
Sparse Core Ops, SparseCore 0:
  12.1 144.7 all-reduce.8
  428.6 185.2 all-reduce.10
  618.8 138.9 all-reduce.12
  1020.6 186.9 all-reduce.14
  1212.9 140.1 all-reduce.16
where the time goes:
time: 1570 us; the launch traced here: 1560 us
  waiting for transfers between devices  876 us (56%)
  other arithmetic  300 us (19%)
  local copies, waits for them, and re-layouts  133 us (8%)
  starting transfers between devices  117 us (7%)
  matrix products  91.5 us (6%)
  between operations  37.7 us (2%)
    psum x2, waiting for transfers between devices, on_device(): projected = lax.psum(local_gram(stacked, image), ('wide', 'col'))  370 us
    psum x2, waiting for transfers between devices, on_device(): gram_sum = lax.psum(local_gram(image, image), ('wide', 'col'))  270 us
    psum x1, waiting for transfers between devices, on_device(): first_sum = lax.psum(local_gram(rhs, rhs), ('wide', 'col'))  147 us
    ppermute x34, starting transfers between devices, passed_along(): return lax.ppermute(block, axis, route)  94.5 us
    another operation x15, other arithmetic, on_device(): small_factor = jnp.linalg.cholesky(normal_matrix)  79.5 us
    another operation x14, other arithmetic, on_device(): factor = jnp.linalg.cholesky(gram_sum)  76.6 us
    ppermute x4, waiting for transfers between devices, with_halo(): lax.ppermute(lax.slice_in_dim(block, block.shape[dim] - width, None, axis...  49.5 us
    another operation x4, other arithmetic, lower_solve(): lax.linalg.triangular_solve(factor, matrix, left_side=False, lower=True,...  42.9 us
  transfers between devices with their start and end apart: 47, of which 22 were waited for; matrix products, arithmetic and copies ran while one was open for 7% of the time, Pallas kernels for 0%

commit v1 on v0

--- a/solution.py
+++ b/solution.py
@@ -144,7 +144,7 @@
     schwarz_inverse,
 ):
     width = rhs.shape[1]
-    first_sum = lax.psum(local_gram(rhs, rhs), ("wide", "col"))
+    first_sum = jnp.sum(lax.all_gather(local_gram(rhs, rhs), ("wide", "col")), axis=0)
     factor = jnp.linalg.cholesky(first_sum)
     beta_block = factor.T
     bases = [lower_solve(factor, rhs)]

time: 1570 us -> 1550 us (0.987)
  waiting for transfers between devices: 876 us -> 841 us
    psum x1 -> x0, waiting for transfers between devices: 147 us -> none  [on_device(): first_sum = lax.psum(local_gram(rhs, rhs), ('wide', 'col'))]
    all_gather x0 -> x1, waiting for transfers between devices: none -> 111 us  [on_device(): lax.all_gather(local_gram(rhs, rhs), ('wide', 'col'))]
where the time goes in v1:
time: 1550 us; the launch traced here: 1530 us
  waiting for transfers between devices  841 us (54%)
  other arithmetic  313 us (20%)
  local copies, waits for them, and re-layouts  133 us (9%)
  starting transfers between devices  116 us (7%)
  matrix products  91.5 us (6%)
  between operations  37.6 us (2%)
    psum x2, waiting for transfers between devices, on_device(): projected = lax.psum(local_gram(stacked, image), ('wide', 'col'))  371 us
    psum x2, waiting for transfers between devices, on_device(): gram_sum = lax.psum(local_gram(image, image), ('wide', 'col'))  270 us
    all_gather x1, waiting for transfers between devices, on_device(): lax.all_gather(local_gram(rhs, rhs), ('wide', 'col'))  111 us
    ppermute x34, starting transfers between devices, passed_along(): return lax.ppermute(block, axis, route)  93.9 us
    another operation x15, other arithmetic, on_device(): small_factor = jnp.linalg.cholesky(normal_matrix)  79.5 us
    another operation x14, other arithmetic, on_device(): factor = jnp.linalg.cholesky(gram_sum)  76.6 us
    ppermute x4, waiting for transfers between devices, with_halo(): lax.ppermute(lax.slice_in_dim(block, block.shape[dim] - width, None, axis...  48.1 us
    another operation x4, other arithmetic, lower_solve(): lax.linalg.triangular_solve(factor, matrix, left_side=False, lower=True,...  43.4 us
  transfers between devices with their start and end apart: 47, of which 22 were waited for; matrix products, arithmetic and copies ran while one was open for 7% of the time, Pallas kernels for 0%

profile of v1, /device:TPU:1, one launch (start us, length us, event | category | flops | bytes accessed | tf_op | source)
XLA Modules:
  0.0 1532.5 jit_solution(8782767550591774725)
XLA Ops:
  10.3 110.6 %all-gather.3.cloned.1.call-done = f32[32768,256]{1,0:T(8,128)} async-done(((f32[256,256]{1,0:T(8,128)}), f32[32768,256]{1,0:T(8,128)}) %all-gather.3.cloned.1.call-update) | async-done | bytes 33554448 | tf_op jit(solution)/shard_map/all_gather | solution.py:147
  120.9 12.0 reduce_sum.16
  135.4 11.7 cholesky.392
  147.8 10.4 custom-call.47
  161.9 13.2 cholesky.402
  179.4 6.9 while.36
  186.3 21.5 %custom-call.48 = f32[2,128,128]{1,2,0:T(8,128)} custom-call(f32[2,128,128]{2,1,0:T(8,128)} %get-tuple-element.295), custom_call_target="InvertDiagBlocksLowerTriangular" | custom-call | tf_op jit(solution)/shard_map/triangular_solve/custom-call.9 | solution.py:42
  238.0 4.7 collective-permute-start.5
  258.5 6.1 collective-permute-start.10
  284.6 8.2 collective-permute-start.16
  315.4 17.6 %collective-permute-done.6 = bf16[1,1,768,256]{2,3,1,0:T(8,128)(2,1)} collective-permute-done((bf16[1,1,768,256]{2,3,1,0:T(8,128)(2,1)}, bf16[1,1,768,256]{2,3,1,0:T(8,128)(2,1)}, u32[]{:S(2)}, u32[]{:S(2)}) %collective-permute-start.6) | collective-permute-done | bytes 393248 | tf_op jit(solution)/shard_map/ppermute | solution.py:23
  342.0 5.0 collective-permute-start.8
  362.7 9.3 copy.27
  372.7 14.7 while.33
  372.8 4.4 gather_fusion
  380.2 4.4 gather_fusion
  403.4 186.8 %all-reduce.8.cloned.1.call-done = f32[256,256]{1,0:T(8,128)} async-done(((f32[256,256]{1,0:T(8,128)}), f32[256,256]{1,0:T(8,128)}) %all-reduce.8.cloned.1.call-update) | async-done | bytes 262160 | tf_op jit(solution)/shard_map/psum | solution.py:157
  595.2 138.9 %all-reduce.10.cloned.1.call-done = f32[256,256]{0,1:T(8,128)} async-done(((f32[256,256]{0,1:T(8,128)}), f32[256,256]{0,1:T(8,128)}) %all-reduce.10.cloned.1.call-update) | async-done | bytes 262160 | tf_op jit(solution)/shard_map/psum | solution.py:159
  738.3 13.2 cholesky.419
  754.5 11.3 custom-call.49
  769.2 13.2 cholesky.429
  789.0 7.5 while.37
  796.5 21.1 %custom-call.50 = f32[2,128,128]{1,2,0:T(8,128)} custom-call(f32[2,128,128]{2,1,0:T(8,128)} %get-tuple-element.296), custom_call_target="InvertDiagBlocksLowerTriangular" | custom-call | tf_op jit(solution)/shard_map/triangular_solve/custom-call.9 | solution.py:42
  826.8 6.0 collective-permute-done.22
  839.4 4.4 collective-permute-start.25
  851.4 9.7 collective-permute-start.30
  872.8 4.8 collective-permute-done.34
  881.1 8.3 collective-permute-start.36
  899.1 30.5 %collective-permute-done.26 = bf16[1,1,768,256]{2,3,1,0:T(8,128)(2,1)S(1)} collective-permute-done((bf16[1,1,768,256]{2,3,1,0:T(8,128)(2,1)S(1)}, bf16[1,1,768,256]{2,3,1,0:T(8,128)(2,1)S(1)}, u32[]{:S(2)}, u32[]{:S(2)}) %collective-permute-start.26) | collective-permute-done | bytes 393248 | tf_op jit(solution)/shard_map/ppermute | solution.py:23
  937.4 5.0 collective-permute-start.28
  959.3 9.3 copy.33
  969.3 12.1 while.34
  999.5 184.4 %all-reduce.12.cloned.1.call-done = f32[512,256]{1,0:T(8,128)} async-done(((f32[512,256]{1,0:T(8,128)}), f32[512,256]{1,0:T(8,128)}) %all-reduce.12.cloned.1.call-update) | async-done | bytes 524304 | tf_op jit(solution)/shard_map/psum | solution.py:157
  1191.7 6.2 scatter.16
  1197.9 131.4 %all-reduce.14.cloned.1.call-done = f32[256,256]{0,1:T(8,128)} async-done(((f32[256,256]{0,1:T(8,128)}), f32[256,256]{0,1:T(8,128)}) %all-reduce.14.cloned.1.call-update) | async-done | bytes 262160 | tf_op jit(solution)/shard_map/psum | solution.py:159
  1331.4 11.7 cholesky.446
  1343.2 9.8 custom-call.51
  1353.5 11.7 cholesky.456
  1373.9 11.7 cholesky.167
  1385.8 9.8 custom-call.37
  1398.1 11.9 cholesky.190
  1411.4 9.8 custom-call.38
  1422.8 11.7 cholesky.294
  1435.2 9.8 custom-call.52
  1446.4 11.9 cholesky.307
  1461.7 10.6 while.35
  1472.3 40.2 %custom-call.39 = f32[4,128,128]{1,2,0:T(8,128)S(1)} custom-call(f32[4,128,128]{2,1,0:T(8,128)} %get-tuple-element.288), custom_call_target="InvertDiagBlocksLowerTriangular" | custom-call | tf_op jit(solution)/shard_map/triangular_solve | solution.py:178
  1520.9 4.9 fusion.36
  (392 shorter events, 315.8 us)
Async XLA Ops:
  6.5 114.4 %all-gather.3.cloned.1.call-start = ((), (), s32[]{:S(2)}) async-start(), calls=%async_computation.4 | async-start | bytes 33816576 | tf_op jit(solution)/shard_map/all_gather | solution.py:147
  10.2 580.0 %all-reduce.8.cloned.1.call-start = ((), (), s32[]{:S(2)}) async-start(), calls=%async_computation | async-start | bytes 524288 | tf_op jit(solution)/shard_map/psum | solution.py:157
  213.6 17.0 %collective-permute-start = (bf16[768,256]{0,1:T(8,128)(2,1)}, bf16[768,256]{0,1:T(8,128)(2,1)}, u32[]{:S(2)}, u32[]{:S(2)}) collective-permute-start(bf16[768,256]{0,1:T(8,128)(2,1)} %fusion.109), channel_id=1, source_target_pairs={{0,1},{1,2},{2,3},{3,4},{4,5},{5,6},{6,7},{7,8},{8,9},{9,10},{10,1... | collective-permute-start | bytes 1179656 | tf_op jit(solution)/shard_map/ppermute | solution.py:15
  217.5 14.1 collective-permute-start.2
  218.8 6.5 collective-permute-start.1
  222.8 7.0 collective-permute-start.3
  236.7 11.3 collective-permute-start.4
  238.0 14.9 collective-permute-start.5
  258.5 13.1 collective-permute-start.10
  264.6 9.0 collective-permute-start.11
  265.9 8.4 collective-permute-start.12
  269.0 7.2 collective-permute-start.13
  270.3 9.6 collective-permute-start.14
  271.6 12.3 collective-permute-start.15
  284.6 54.0 %collective-permute-start.16 = (bf16[7,256,256]{1,2,0:T(8,128)(2,1)}, bf16[7,256,256]{1,2,0:T(8,128)(2,1)}, u32[]{:S(2)}, u32[]{:S(2)}) collective-permute-start(bf16[7,256,256]{1,2,0:T(8,128)(2,1)} %bitcast_dynamic-update-slice_fusion.25), channel_id=1, source_target_pairs={{0,48},{16,64},{32,80},{48,96},{64,112},{1,49},{17,65},{33,81},{49... | collective-permute-start | bytes 2752520 | tf_op jit(solution)/shard_map/ppermute | solution.py:15
  292.8 49.3 %collective-permute-start.17 = (bf16[7,256,256]{1,2,0:T(8,128)(2,1)}, bf16[7,256,256]{1,2,0:T(8,128)(2,1)}, u32[]{:S(2)}, u32[]{:S(2)}) collective-permute-start(bf16[7,256,256]{1,2,0:T(8,128)(2,1)} %bitcast_dynamic-update-slice_fusion.25), channel_id=1, source_target_pairs={{0,32},{16,48},{32,64},{48,80},{64,96},{80,112},{1,33},{17,49},{33... | collective-permute-start | bytes 2752520 | tf_op jit(solution)/shard_map/ppermute | solution.py:15
  295.8 37.2 %collective-permute-start.6 = (bf16[1,1,768,256]{2,3,1,0:T(8,128)(2,1)}, bf16[1,1,768,256]{2,3,1,0:T(8,128)(2,1)}, u32[]{:S(2)}, u32[]{:S(2)}) collective-permute-start(bf16[1,1,768,256]{2,3,1,0:T(8,128)(2,1)} %convert_bitcast_fusion.1), channel_id=1, source_target_pairs={{0,16},{16,32},{32,48},{48,64},{64,80},{80,96},{96,112},{1,17},{17... | collective-permute-start | bytes 1179656 | tf_op jit(solution)/shard_map/ppermute | solution.py:23
  297.7 37.2 %collective-permute-start.7 = (bf16[1,1,768,256]{2,3,1,0:T(8,128)(2,1)}, bf16[1,1,768,256]{2,3,1,0:T(8,128)(2,1)}, u32[]{:S(2)}, u32[]{:S(2)}) collective-permute-start(bf16[1,1,768,256]{2,3,1,0:T(8,128)(2,1)} %convert_bitcast_fusion.1), channel_id=1, source_target_pairs={{16,0},{32,16},{48,32},{64,48},{80,64},{96,80},{112,96},{17,1},{33... | collective-permute-start | bytes 1179656 | tf_op jit(solution)/shard_map/ppermute | solution.py:26
  300.9 48.4 %collective-permute-start.18 = (bf16[7,256,256]{1,2,0:T(8,128)(2,1)}, bf16[7,256,256]{1,2,0:T(8,128)(2,1)}, u32[]{:S(2)}, u32[]{:S(2)}) collective-permute-start(bf16[7,256,256]{1,2,0:T(8,128)(2,1)} %bitcast_dynamic-update-slice_fusion.25), channel_id=1, source_target_pairs={{0,16},{16,32},{32,48},{48,64},{64,80},{80,96},{96,112},{1,17},{17... | collective-permute-start | bytes 2752520 | tf_op jit(solution)/shard_map/ppermute | solution.py:15
  333.0 23.7 %collective-permute-start.19 = (bf16[7,256,256]{1,2,0:T(8,128)(2,1)}, bf16[7,256,256]{1,2,0:T(8,128)(2,1)S(1)}, u32[]{:S(2)}, u32[]{:S(2)}) collective-permute-start(bf16[7,256,256]{1,2,0:T(8,128)(2,1)} %bitcast_dynamic-update-slice_fusion.25), channel_id=1, source_target_pairs={{16,0},{32,16},{48,32},{64,48},{80,64},{96,80},{112,96},{17,1},{33... | collective-permute-start | bytes 2752520 | tf_op jit(solution)/shard_map/ppermute | solution.py:15
  334.9 25.7 %collective-permute-start.20 = (bf16[7,256,256]{1,2,0:T(8,128)(2,1)}, bf16[7,256,256]{1,2,0:T(8,128)(2,1)S(1)}, u32[]{:S(2)}, u32[]{:S(2)}) collective-permute-start(bf16[7,256,256]{1,2,0:T(8,128)(2,1)} %bitcast_dynamic-update-slice_fusion.25), channel_id=1, source_target_pairs={{32,0},{48,16},{64,32},{80,48},{96,64},{112,80},{33,1},{49,17},{65... | collective-permute-start | bytes 2752520 | tf_op jit(solution)/shard_map/ppermute | solution.py:15
  338.6 23.0 %collective-permute-start.21 = (bf16[7,256,256]{1,2,0:T(8,128)(2,1)}, bf16[7,256,256]{1,2,0:T(8,128)(2,1)S(1)}, u32[]{:S(2)}, u32[]{:S(2)}) collective-permute-start(bf16[7,256,256]{1,2,0:T(8,128)(2,1)} %bitcast_dynamic-update-slice_fusion.25), channel_id=1, source_target_pairs={{48,0},{64,16},{80,32},{96,48},{112,64},{49,1},{65,17},{81,33},{97... | collective-permute-start | bytes 2752520 | tf_op jit(solution)/shard_map/ppermute | solution.py:15
  342.0 45.4 %collective-permute-start.8 = (bf16[3,1,768,256]{2,3,1,0:T(8,128)(2,1)}, bf16[3,1,768,256]{2,3,1,0:T(8,128)(2,1)}, u32[]{:S(2)}, u32[]{:S(2)}) collective-permute-start(bf16[3,1,768,256]{2,3,1,0:T(8,128)(2,1)} %pad_maximum_fusion.2), channel_id=1, source_target_pairs={{0,1},{1,2},{2,3},{3,4},{4,5},{5,6},{6,7},{7,8},{8,9},{9,10},{10,1... | collective-permute-start | bytes 3538952 | tf_op jit(solution)/shard_map/ppermute | solution.py:23
  349.3 38.2 %collective-permute-start.9 = (bf16[3,1,768,256]{2,3,1,0:T(8,128)(2,1)}, bf16[3,1,768,256]{2,3,1,0:T(8,128)(2,1)}, u32[]{:S(2)}, u32[]{:S(2)}) collective-permute-start(bf16[3,1,768,256]{2,3,1,0:T(8,128)(2,1)} %pad_maximum_fusion.2), channel_id=1, source_target_pairs={{1,0},{2,1},{3,2},{4,3},{5,4},{6,5},{7,6},{8,7},{9,8},{10,9},{11,1... | collective-permute-start | bytes 3538952 | tf_op jit(solution)/shard_map/ppermute | solution.py:26
  403.3 385.6 %copy-start.38 = (s32[2,2]{1,0:T(2,128)S(1)}, s32[2,2]{1,0:T(2,128)}, u32[]{:S(2)}) copy-start(s32[2,2]{1,0:T(2,128)} %copy-done.37) | copy-start | bytes 52
  403.3 330.8 %all-reduce.10.cloned.1.call-start = ((), (), s32[]{:S(2)}) async-start(), calls=%async_computation.1 | async-start | bytes 524288 | tf_op jit(solution)/shard_map/psum | solution.py:159
  595.0 588.9 %all-reduce.12.cloned.1.call-start = ((), (), s32[]{:S(2)}) async-start(), calls=%async_computation.2 | async-start | bytes 1048576 | tf_op jit(solution)/shard_map/psum | solution.py:157
  822.9 9.9 collective-permute-start.22
  825.5 11.2 collective-permute-start.23
  837.9 8.4 collective-permute-start.24
  839.4 9.3 collective-permute-start.25
  851.4 16.7 %collective-permute-start.30 = (bf16[256,256]{0,1:T(8,128)(2,1)S(1)}, bf16[256,256]{0,1:T(8,128)(2,1)S(1)}, u32[]{:S(2)}, u32[]{:S(2)}) collective-permute-start(bf16[256,256]{0,1:T(8,128)(2,1)S(1)} %bitcast.420), channel_id=1, source_target_pairs={{0,3},{1,4},{2,5},{3,6},{4,7},{5,8},{6,9},{7,10},{8,11},{9,12},{10... | collective-permute-start | bytes 393224 | tf_op jit(solution)/shard_map/ppermute | solution.py:15
  861.1 9.0 collective-permute-start.31
  862.7 8.1 collective-permute-start.32
  865.5 6.7 collective-permute-start.33
  866.8 10.8 collective-permute-start.34
  868.1 12.3 collective-permute-start.35
  881.1 52.9 %collective-permute-start.36 = (bf16[7,256,256]{1,2,0:T(8,128)(2,1)}, bf16[7,256,256]{1,2,0:T(8,128)(2,1)}, u32[]{:S(2)}, u32[]{:S(2)}) collective-permute-start(bf16[7,256,256]{1,2,0:T(8,128)(2,1)} %bitcast_dynamic-update-slice_fusion.19), channel_id=1, source_target_pairs={{0,48},{16,64},{32,80},{48,96},{64,112},{1,49},{17,65},{33,81},{49... | collective-permute-start | bytes 2752520 | tf_op jit(solution)/shard_map/ppermute | solution.py:15
  889.4 48.1 %collective-permute-start.37 = (bf16[7,256,256]{1,2,0:T(8,128)(2,1)}, bf16[7,256,256]{1,2,0:T(8,128)(2,1)}, u32[]{:S(2)}, u32[]{:S(2)}) collective-permute-start(bf16[7,256,256]{1,2,0:T(8,128)(2,1)} %bitcast_dynamic-update-slice_fusion.19), channel_id=1, source_target_pairs={{0,32},{16,48},{32,64},{48,80},{64,96},{80,112},{1,33},{17,49},{33... | collective-permute-start | bytes 2752520 | tf_op jit(solution)/shard_map/ppermute | solution.py:15
  891.6 38.0 %collective-permute-start.26 = (bf16[1,1,768,256]{2,3,1,0:T(8,128)(2,1)S(1)}, bf16[1,1,768,256]{2,3,1,0:T(8,128)(2,1)S(1)}, u32[]{:S(2)}, u32[]{:S(2)}) collective-permute-start(bf16[1,1,768,256]{2,3,1,0:T(8,128)(2,1)S(1)} %convert_bitcast_fusion), channel_id=1, source_target_pairs={{0,16},{16,32},{32,48},{48,64},{64,80},{80,96},{96,112},{1,17},{17... | collective-permute-start | bytes 1179656 | tf_op jit(solution)/shard_map/ppermute | solution.py:23
  893.5 38.0 %collective-permute-start.27 = (bf16[1,1,768,256]{2,3,1,0:T(8,128)(2,1)S(1)}, bf16[1,1,768,256]{2,3,1,0:T(8,128)(2,1)S(1)}, u32[]{:S(2)}, u32[]{:S(2)}) collective-permute-start(bf16[1,1,768,256]{2,3,1,0:T(8,128)(2,1)S(1)} %convert_bitcast_fusion), channel_id=1, source_target_pairs={{16,0},{32,16},{48,32},{64,48},{80,64},{96,80},{112,96},{17,1},{33... | collective-permute-start | bytes 1179656 | tf_op jit(solution)/shard_map/ppermute | solution.py:26
  896.0 48.7 %collective-permute-start.38 = (bf16[7,256,256]{1,2,0:T(8,128)(2,1)}, bf16[7,256,256]{1,2,0:T(8,128)(2,1)}, u32[]{:S(2)}, u32[]{:S(2)}) collective-permute-start(bf16[7,256,256]{1,2,0:T(8,128)(2,1)} %bitcast_dynamic-update-slice_fusion.19), channel_id=1, source_target_pairs={{0,16},{16,32},{32,48},{48,64},{64,80},{80,96},{96,112},{1,17},{17... | collective-permute-start | bytes 2752520 | tf_op jit(solution)/shard_map/ppermute | solution.py:15
  929.6 23.7 %collective-permute-start.39 = (bf16[7,256,256]{1,2,0:T(8,128)(2,1)}, bf16[7,256,256]{1,2,0:T(8,128)(2,1)S(1)}, u32[]{:S(2)}, u32[]{:S(2)}) collective-permute-start(bf16[7,256,256]{1,2,0:T(8,128)(2,1)} %bitcast_dynamic-update-slice_fusion.19), channel_id=1, source_target_pairs={{16,0},{32,16},{48,32},{64,48},{80,64},{96,80},{112,96},{17,1},{33... | collective-permute-start | bytes 2752520 | tf_op jit(solution)/shard_map/ppermute | solution.py:15
  931.5 25.7 %collective-permute-start.40 = (bf16[7,256,256]{1,2,0:T(8,128)(2,1)}, bf16[7,256,256]{1,2,0:T(8,128)(2,1)S(1)}, u32[]{:S(2)}, u32[]{:S(2)}) collective-permute-start(bf16[7,256,256]{1,2,0:T(8,128)(2,1)} %bitcast_dynamic-update-slice_fusion.19), channel_id=1, source_target_pairs={{32,0},{48,16},{64,32},{80,48},{96,64},{112,80},{33,1},{49,17},{65... | collective-permute-start | bytes 2752520 | tf_op jit(solution)/shard_map/ppermute | solution.py:15
  934.0 24.2 %collective-permute-start.41 = (bf16[7,256,256]{1,2,0:T(8,128)(2,1)}, bf16[7,256,256]{1,2,0:T(8,128)(2,1)S(1)}, u32[]{:S(2)}, u32[]{:S(2)}) collective-permute-start(bf16[7,256,256]{1,2,0:T(8,128)(2,1)} %bitcast_dynamic-update-slice_fusion.19), channel_id=1, source_target_pairs={{48,0},{64,16},{80,32},{96,48},{112,64},{49,1},{65,17},{81,33},{97... | collective-permute-start | bytes 2752520 | tf_op jit(solution)/shard_map/ppermute | solution.py:15
  937.4 44.0 %collective-permute-start.28 = (bf16[3,1,768,256]{2,3,1,0:T(8,128)(2,1)}, bf16[3,1,768,256]{2,3,1,0:T(8,128)(2,1)}, u32[]{:S(2)}, u32[]{:S(2)}) collective-permute-start(bf16[3,1,768,256]{2,3,1,0:T(8,128)(2,1)} %pad_maximum_fusion.3), channel_id=1, source_target_pairs={{0,1},{1,2},{2,3},{3,4},{4,5},{5,6},{6,7},{7,8},{8,9},{9,10},{10,1... | collective-permute-start | bytes 3538952 | tf_op jit(solution)/shard_map/ppermute | solution.py:23
  944.7 36.7 %collective-permute-start.29 = (bf16[3,1,768,256]{2,3,1,0:T(8,128)(2,1)}, bf16[3,1,768,256]{2,3,1,0:T(8,128)(2,1)}, u32[]{:S(2)}, u32[]{:S(2)}) collective-permute-start(bf16[3,1,768,256]{2,3,1,0:T(8,128)(2,1)} %pad_maximum_fusion.3), channel_id=1, source_target_pairs={{1,0},{2,1},{3,2},{4,3},{5,4},{6,5},{7,6},{8,7},{9,8},{10,9},{11,1... | collective-permute-start | bytes 3538952 | tf_op jit(solution)/shard_map/ppermute | solution.py:26
  996.7 332.6 %all-reduce.14.cloned.1.call-start = ((), (), s32[]{:S(2)}) async-start(), calls=%async_computation.3 | async-start | bytes 524288 | tf_op jit(solution)/shard_map/psum | solution.py:159
  (44 other events, 947.7 us)
Sparse Core Ops, SparseCore 0:
  10.5 110.3 all-gather.2
  403.4 186.7 all-reduce.7
  595.1 138.9 all-reduce.9
  996.8 186.9 all-reduce.11
  1189.2 140.1 all-reduce.13
